TPU v7x, 256 devices: a whole 4x4x8 slice. The times are simulated.
256 devices in a mesh: dom: 32 (over z, y), grp: 8 (over x, core).
Axes of the slice: x: 4, y: 4, z: 8, core: 2. Of those that a mesh axis runs over, the one named last changes fastest.
Arguments:
- deflation: bfloat16 [256, 1024, 3, 2, 128], P(('dom', 'grp')), may hold values from -1.5 to 1.5
- inverse: bfloat16 [256, 2, 1024, 1024], P(('dom', 'grp'))
- operator: bfloat16 [256, 2, 1024, 1024], P(('dom', 'grp'))
- neighbours: int32 [256, 6], P(('dom', 'grp')), may hold values from -1 to 255, as said below
- counts: int32 [256, 6], P(('dom', 'grp')), may hold values from 0 to 256, as said below
- margin_rows: int32 [256, 6, 256], P(('dom', 'grp')), may hold values from 0 to 1023, as said below
- owners: int32 [256, 6, 1], P(('dom', 'grp')), may hold values from 0 to 7; in each aligned block of 6 rows (0 to 5, 6 to 11, ..., all dimensions but the last counted through in order) no two rows name the same one
Outputs:
- owned_blocks: float32 [2048, 3, 2, 128, 128], P(('dom', 'grp'))
Inputs may be any that keep to these rules, and one draw needn't show every extreme that they name: `neighbours`: entry n of a subdomain's list is the subdomain with the same group index whose dom index is d + o_n modulo 32 (o_n = -3, -2, -1, 1, 2, 3), or -1 where that pair shares no rows; the relation is symmetric. `counts`: equal on both sides of a pair, 0 exactly where the list holds -1, and 256 for some pair in every draw. `margin_rows`: distinct within each slot; for k below the pair's count, entry k on one side and entry k on the other side name the same global edge. `owners`: among one subdomain's 6 blocks no group index is named more than 1 times; some subdomain names one exactly 1 times.
All inputs are finite; a program needn't handle non-finite values.
Results may differ from a plain program's by a relative error of at most 0.0048.
Values may be sent and summed in bfloat16 or wider, within the bound.
A program may use at most 64 MiB of HBM per device.

v0:
```python
import jax
import jax.numpy as jnp
from jax import lax
from jax.sharding import PartitionSpec as P

OFFSETS = (-3, -2, -1, 1, 2, 3)


def passed_along(value, axis, steps):
    count = lax.axis_size(axis)
    pairs = [(source, (source + steps) % count) for source in range(count)]
    return lax.ppermute(value, axis, pairs)


def complex_apply(matrix, vectors):
    edges = vectors.shape[0]
    flat = vectors.reshape(edges, -1)
    real_part = jnp.dot(matrix[0], flat, preferred_element_type=jnp.float32).reshape(vectors.shape)
    imag_part = jnp.dot(matrix[1], flat, preferred_element_type=jnp.float32).reshape(vectors.shape)
    result_real = real_part[:, :, 0] - imag_part[:, :, 1]
    result_imag = real_part[:, :, 1] + imag_part[:, :, 0]
    return jnp.stack([result_real, result_imag], axis=2).astype(jnp.bfloat16)


def on_device(deflation, inverse, operator, neighbours, counts, margin_rows, owners):
    set_count = deflation.shape[2]
    width = deflation.shape[4]
    margin = margin_rows.shape[2]
    slots = margin_rows.shape[1]
    vectors = deflation[0]
    first_pass = complex_apply(inverse[0], vectors)
    second_pass = complex_apply(inverse[0], first_pass)
    imaged = complex_apply(operator[0], second_pass)
    slot_rows = margin_rows[0]
    positions = jnp.arange(margin, dtype=jnp.int32)
    live = (neighbours[0][:, None] >= 0) & (positions[None, :] < counts[0][:, None])
    outgoing = jnp.where(
        live[:, :, None, None, None], imaged[slot_rows], jnp.zeros((), jnp.bfloat16)
    )
    pieces = [None] * len(OFFSETS)
    for slot_index, offset in enumerate(OFFSETS):
        pieces[len(OFFSETS) - 1 - slot_index] = passed_along(outgoing[slot_index], "dom", offset)
    incoming = jnp.stack(pieces).reshape(slots, margin, set_count, 2 * width)
    projector = vectors[slot_rows].reshape(slots, margin, set_count, 2 * width)
    gram = jnp.einsum("nrsk,nrsl->nskl", projector, incoming, preferred_element_type=jnp.float32)
    real_part = gram[:, :, :width, :width] - gram[:, :, width:, width:]
    imag_part = gram[:, :, :width, width:] + gram[:, :, width:, :width]
    coupling = jnp.stack([real_part, imag_part], axis=2)
    group_count = lax.axis_size("grp")
    capacity = (slots + group_count - 1) // group_count
    targets_grp = owners[0, :, 0]
    same = targets_grp[:, None] == targets_grp[None, :]
    slot_ids = jnp.arange(slots, dtype=jnp.int32)
    earlier = slot_ids[None, :] < slot_ids[:, None]
    rank = jnp.sum((same & earlier).astype(jnp.int32), axis=1)
    place = targets_grp * capacity + rank
    holders = jnp.arange(group_count * capacity, dtype=jnp.int32)
    selector = (holders[:, None] == place[None, :]).astype(jnp.float32)
    packed_blocks = jnp.einsum(
        "pn,nwxyz->pwxyz", selector, coupling, precision=lax.Precision.HIGHEST
    )
    return lax.all_to_all(packed_blocks, "grp", split_axis=0, concat_axis=0, tiled=True)


def solution(mesh):
    placed = (
        P(("dom", "grp"), None, None, None, None),
        P(("dom", "grp"), None, None, None),
        P(("dom", "grp"), None, None, None),
        P(("dom", "grp"), None),
        P(("dom", "grp"), None),
        P(("dom", "grp"), None, None),
        P(("dom", "grp"), None, None),
    )
    return jax.shard_map(
        on_device,
        mesh=mesh,
        in_specs=placed,
        out_specs=P(("dom", "grp"), None, None, None, None),
        check_vma=False,
    )
```

profile of v0, /device:TPU:16, one launch (start us, length us, event | category | flops | bytes accessed | tf_op | source)
XLA Modules:
  0.0 205.4 jit_solution(16852329558391769799)
XLA Ops:
  0.0 3.9 %reshape_squeeze.3 = bf16[1024,768]{1,0:T(8,128)(2,1)S(1)} reshape(bf16[1,1024,3,2,128]{4,3,2,1,0:T(2,128)(2,1)} %param.7) | data formatting | bytes 3145728 | tf_op jit(solution)/shard_map/reshape;squeeze | solution.py:17
  3.9 0.9 copy.46
  4.9 0.0 copy-start.6
  4.9 3.6 %fusion.4 = f32[1024,3,2,128]{0,3,2,1:T(8,128)S(1)} fusion(bf16[3,2,128,1024]{3,2,1,0:T(8,128)(2,1)S(1)} %bitcast.100, bf16[1,2,1024,1024]{3,2,1,0:T(8,128)(2,1)} %param.8), kind=kOutput, calls=%fused_computation.8 | convolution fusion | flops 1610612736 | bytes 6815744 | tf_op jit(solution)/shard_map/dot_general | solution.py:19
  8.4 1.8 fusion.6
  10.3 0.8 fusion.25
  11.1 0.1 pad_maximum_fusion.1
  11.3 1.8 fusion.14
  13.1 1.8 fusion.12
  14.9 0.0 copy-start.7
  15.0 0.8 fusion.23
  15.8 0.1 pad_maximum_fusion.2
  16.0 1.2 copy-done.7
  17.1 1.8 fusion.10
  19.0 3.5 %fusion.8 = f32[768,1024]{1,0:T(8,128)} fusion(bf16[1024,768]{0,1:T(8,128)(2,1)S(1)} %bitcast.99, bf16[1,2,1024,1024]{3,2,1,0:T(8,128)(2,1)S(1)} %copy-done.7), kind=kOutput, calls=%fused_computation.12 | convolution fusion | flops 1610612736 | bytes 6815744 | tf_op jit(solution)/shard_map/dot_general | solution.py:19
  22.5 1.4 fusion.35
  23.9 1.7 copy.68
  25.6 3.9 %fusion.34 = (f32[1024,3,1,128]{0,3,2,1:T(8,128)}, f32[1024,3,1,128]{0,3,2,1:T(8,128)}) fusion(f32[1024,3,2,128]{0,3,2,1:T(8,128)} %bitcast.92), kind=kLoop, calls=%fused_computation.68 | loop fusion | bytes 6291456 | tf_op jit(solution)/shard_map/slice | solution.py:20
  29.5 4.0 %copy.69 = f32[1024,3,1,128]{3,2,1,0:T(1,128)S(1)} copy(f32[1024,3,1,128]{0,3,2,1:T(8,128)} %get-tuple-element.11) | data formatting | bytes 3145728
  33.5 4.8 %copy.70 = f32[1024,3,1,128]{3,2,1,0:T(1,128)} copy(f32[1024,3,1,128]{0,3,2,1:T(8,128)} %get-tuple-element.14) | data formatting | bytes 3145728
  38.3 4.9 %copy.71 = f32[1024,3,1,128]{3,2,1,0:T(1,128)} copy(f32[1024,3,1,128]{0,3,2,1:T(8,128)} %get-tuple-element.12) | data formatting | bytes 3145728
  43.3 4.6 %add_convert_fusion = (bf16[1024,3,1,128]{3,2,1,0:T(2,128)(2,1)S(1)}, bf16[1024,3,1,128]{3,2,1,0:T(2,128)(2,1)S(1)}) fusion(f32[1024,3,1,128]{3,2,1,0:T(1,128)} %copy.70, f32[1024,3,1,128]{3,2,1,0:T(1,128)} %copy.71, f32[1024,3,1,128]{3,2,1,0:T(1,128)S(1)} %copy.68, f32[1024,3,1,128]{3,2,1,0:T(1,128)S(1)} %copy.69), kind=kLoop, calls=%fused_computation.37 | loop fusion | flops 1572864 | bytes 7864320 | tf_op jit(solution)/shard_map/convert.1
  47.9 3.6 %pad_maximum_fusion.3 = bf16[1024,3,2,128]{3,2,1,0:T(2,128)(2,1)S(1)} fusion(bf16[1024,3,1,128]{3,2,1,0:T(2,128)(2,1)S(1)} %get-tuple-element.21, bf16[1024,3,1,128]{3,2,1,0:T(2,128)(2,1)S(1)} %get-tuple-element.22), kind=kLoop, calls=%fused_computation.36 | loop fusion | flops 3145728 | bytes 3145728 | tf_op jit(solution)/shard_map/stack | solution.py:22
  51.6 8.1 %gather_fusion.1 = bf16[1536,3,2,128]{3,2,1,0:T(2,128)(2,1)} fusion(bf16[1024,3,2,128]{3,2,1,0:T(2,128)(2,1)S(1)} %pad_maximum_fusion.3, s32[2048]{0:T(1024)S(1)} %pad_clamp_fusion), kind=kCustom, calls=%fused_computation.1 | custom fusion | bytes 4724736 | tf_op jit(solution)/shard_map/gather | solution.py:38
  59.7 2.0 copy.51
  61.8 0.1 fusion.28
  61.8 0.3 broadcast_select_fusion
  62.2 1.3 slice_bitcast_fusion
  63.5 1.8 collective-permute-start
  65.3 2.9 %collective-permute-start.1 = (bf16[256,3,2,128]{3,0,2,1:T(8,128)(2,1)}, bf16[256,3,2,128]{3,0,2,1:T(8,128)(2,1)}, u32[]{:S(2)}, u32[]{:S(2)}) collective-permute-start(bf16[256,3,2,128]{3,0,2,1:T(8,128)(2,1)} %get-tuple-element.19), channel_id=1, source_target_pairs={{0,16},{8,24},{16,32},{24,40},{32,48},{40,56},{48,64},{56,72},{64,... | collective-permute-start | bytes 1179656 | tf_op jit(solution)/shard_map/ppermute | solution.py:12
  68.2 1.0 collective-permute-start.2
  69.2 1.1 collective-permute-start.3
  70.2 3.9 %collective-permute-start.4 = (bf16[256,3,2,128]{3,0,2,1:T(8,128)(2,1)}, bf16[256,3,2,128]{3,0,2,1:T(8,128)(2,1)}, u32[]{:S(2)}, u32[]{:S(2)}) collective-permute-start(bf16[256,3,2,128]{3,0,2,1:T(8,128)(2,1)} %get-tuple-element.16), channel_id=1, source_target_pairs={{0,240},{8,248},{16,0},{24,8},{32,16},{40,24},{48,32},{56,40},{64,... | collective-permute-start | bytes 1179656 | tf_op jit(solution)/shard_map/ppermute | solution.py:12
  74.2 5.9 %collective-permute-done = bf16[256,3,2,128]{3,0,2,1:T(8,128)(2,1)S(1)} collective-permute-done((bf16[256,3,2,128]{3,0,2,1:T(8,128)(2,1)S(1)}, bf16[256,3,2,128]{3,0,2,1:T(8,128)(2,1)S(1)}, u32[]{:S(2)}, u32[]{:S(2)}) %collective-permute-start) | collective-permute-done | bytes 393248 | tf_op jit(solution)/shard_map/ppermute | solution.py:12
  80.1 0.8 copy-done.3
  80.9 27.3 %collective-permute-start.5 = (bf16[256,3,2,128]{3,0,2,1:T(8,128)(2,1)}, bf16[256,3,2,128]{3,0,2,1:T(8,128)(2,1)}, u32[]{:S(2)}, u32[]{:S(2)}) collective-permute-start(bf16[256,3,2,128]{3,0,2,1:T(8,128)(2,1)} %get-tuple-element.15), channel_id=1, source_target_pairs={{0,232},{8,240},{16,248},{24,0},{32,8},{40,16},{48,24},{56,32},{64... | collective-permute-start | bytes 1179656 | tf_op jit(solution)/shard_map/ppermute | solution.py:12
  108.2 0.2 convert_reduce_fusion
  108.4 8.4 %gather_fusion = bf16[1536,3,2,128]{3,2,1,0:T(2,128)(2,1)} fusion(bf16[1024,3,2,128]{3,2,1,0:T(2,128)(2,1)S(1)} %bitcast.89, s32[2048]{0:T(1024)S(1)} %pad_clamp_fusion), kind=kCustom, calls=%fused_computation | custom fusion | bytes 4724736 | tf_op jit(solution)/shard_map/gather | solution.py:44
  116.8 7.4 %reshape.178 = bf16[6,256,3,256]{3,2,1,0:T(4,128)(2,1)S(1)} reshape(bf16[1536,3,2,128]{3,2,1,0:T(2,128)(2,1)} %gather_fusion) | data formatting | bytes 4718592 | tf_op jit(solution)/shard_map/reshape | solution.py:44
  124.2 1.4 copy.52
  125.6 1.0 stack.51
  126.6 2.1 %copy.53 = bf16[256,3,2,128]{3,2,0,1:T(2,128)(2,1)} copy(bf16[256,3,2,128]{3,0,2,1:T(8,128)(2,1)} %collective-permute-done.1) | data formatting | bytes 786432 | tf_op jit(solution)/shard_map/ppermute | solution.py:12
  128.7 1.2 stack.52
  130.0 2.1 %copy.54 = bf16[256,3,2,128]{3,2,0,1:T(2,128)(2,1)} copy(bf16[256,3,2,128]{3,0,2,1:T(8,128)(2,1)} %collective-permute-done.2) | data formatting | bytes 786432 | tf_op jit(solution)/shard_map/ppermute | solution.py:12
  132.1 2.0 stack.53
  134.1 2.1 %copy.55 = bf16[256,3,2,128]{3,2,0,1:T(2,128)(2,1)} copy(bf16[256,3,2,128]{3,0,2,1:T(8,128)(2,1)} %collective-permute-done.3) | data formatting | bytes 786432 | tf_op jit(solution)/shard_map/ppermute | solution.py:12
  136.3 2.0 stack.54
  138.3 2.1 %copy.56 = bf16[256,3,2,128]{3,2,0,1:T(2,128)(2,1)} copy(bf16[256,3,2,128]{3,0,2,1:T(8,128)(2,1)} %collective-permute-done.4) | data formatting | bytes 786432 | tf_op jit(solution)/shard_map/ppermute | solution.py:12
  140.4 2.0 stack.55
  142.4 1.8 constant_dynamic-update-slice_fusion.5
  144.2 2.2 %copy.57 = bf16[256,3,2,128]{3,2,0,1:T(2,128)(2,1)} copy(bf16[256,3,2,128]{3,0,2,1:T(8,128)(2,1)} %collective-permute-done.5) | data formatting | bytes 786432 | tf_op jit(solution)/shard_map/ppermute | solution.py:12
  146.3 2.0 stack.56
  148.3 0.8 constant_dynamic-update-slice_fusion.4
  149.1 1.8 constant_dynamic-update-slice_fusion.3
  150.9 1.8 constant_dynamic-update-slice_fusion.2
  152.6 0.8 constant_dynamic-update-slice_fusion.1
  153.4 0.8 constant_dynamic-update-slice_fusion
  154.2 2.5 %fusion.2 = f32[6,3,256,256]{3,2,1,0:T(8,128)S(1)} fusion(bf16[6,256,3,256]{3,1,2,0:T(8,128)(2,1)} %constant_dynamic-update-slice_fusion, bf16[6,256,3,256]{3,2,1,0:T(4,128)(2,1)S(1)} %reshape.178), kind=kOutput, calls=%fused_computation.5 | convolution fusion | flops 603979776 | bytes 9437184 | tf_op jit(solution)/shard_map/nrsk,nrsl->nskl/dot_general | solution.py:45
  156.7 0.3 fusion.27
  157.0 0.2 pad_maximum_fusion
  157.2 2.9 %fusion = f32[8,3,2,128,128]{4,0,3,2,1:T(8,128)S(1)} fusion(f32[6,3,2,128,128]{4,3,1,0,2:T(8,128)S(1)} %pad_maximum_fusion, s32[6]{0:T(128)S(1)} %bitcast_add_fusion), kind=kOutput, calls=%fused_computation.2 | convolution fusion | flops 56623152 | bytes 5505048 | tf_op jit(solution)/shard_map/pn,nwxyz->pwxyz/dot_general | solution.py:59
  160.0 0.6 copy.60
  160.7 43.0 %all_to_all.5 = f32[8,3,2,128,128]{4,3,2,1,0:T(8,128)S(1)} all-to-all(f32[8,3,2,128,128]{4,3,2,1,0:T(8,128)S(1)} %copy.60), channel_id=1, replica_groups=mesh['dom'=32,'grp'=8] {'grp'}, dimensions={0} | all-to-all | bytes 6291456 | tf_op jit(solution)/shard_map/all_to_all | solution.py:62
  203.7 1.7 copy.82
  (26 shorter events, 0.1 us)
Async XLA Ops:
  4.9 3.6 %copy-start.6 = (bf16[1,2,1024,1024]{3,2,1,0:T(8,128)(2,1)S(1)}, bf16[1,2,1024,1024]{3,2,1,0:T(8,128)(2,1)}, u32[]{:S(2)}) copy-start(bf16[1,2,1024,1024]{3,2,1,0:T(8,128)(2,1)} %param.8) | copy-start | bytes 12582916
  14.9 2.2 %copy-start.7 = (bf16[1,2,1024,1024]{3,2,1,0:T(8,128)(2,1)S(1)}, bf16[1,2,1024,1024]{3,2,1,0:T(8,128)(2,1)}, u32[]{:S(2)}) copy-start(bf16[1,2,1024,1024]{3,2,1,0:T(8,128)(2,1)} %param.9) | copy-start | bytes 12582916
  38.3 4.9 %copy-start.4 = (s32[1,6,256]{2,0,1:T(1,128)S(1)}, s32[1,6,256]{2,0,1:T(1,128)}, u32[]{:S(2)}) copy-start(s32[1,6,256]{2,0,1:T(1,128)} %param.12) | copy-start | bytes 18436
  59.7 2.0 copy-start.8
  59.7 2.0 copy-start.5
  62.2 46.0 %copy-start.9 = (s32[1,6,1]{1,2,0:T(1,128)S(1)}, s32[1,6,1]{1,2,0:T(1,128)}, u32[]{:S(2)}) copy-start(s32[1,6,1]{1,2,0:T(1,128)} %param.13) | copy-start | bytes 76
  62.2 46.2 %copy-start = (bf16[1,1024,3,2,128]{4,3,2,1,0:T(2,128)(2,1)S(1)}, bf16[1,1024,3,2,128]{4,3,2,1,0:T(2,128)(2,1)}, u32[]{:S(2)}) copy-start(bf16[1,1024,3,2,128]{4,3,2,1,0:T(2,128)(2,1)} %param.7) | copy-start | bytes 4718596
  63.5 16.6 %collective-permute-start = (bf16[256,3,2,128]{3,0,2,1:T(8,128)(2,1)S(1)}, bf16[256,3,2,128]{3,0,2,1:T(8,128)(2,1)S(1)}, u32[]{:S(2)}, u32[]{:S(2)}) collective-permute-start(bf16[256,3,2,128]{3,0,2,1:T(8,128)(2,1)S(1)} %get-tuple-element.20), channel_id=1, source_target_pairs={{0,24},{8,32},{16,40},{24,48},{32,56},{40,64},{48,72},{56,80},{64,... | collective-permute-start | bytes 1179656 | tf_op jit(solution)/shard_map/ppermute | solution.py:12
  65.3 61.3 %collective-permute-start.1 = (bf16[256,3,2,128]{3,0,2,1:T(8,128)(2,1)}, bf16[256,3,2,128]{3,0,2,1:T(8,128)(2,1)}, u32[]{:S(2)}, u32[]{:S(2)}) collective-permute-start(bf16[256,3,2,128]{3,0,2,1:T(8,128)(2,1)} %get-tuple-element.19), channel_id=1, source_target_pairs={{0,16},{8,24},{16,32},{24,40},{32,48},{40,56},{48,64},{56,72},{64,... | collective-permute-start | bytes 1179656 | tf_op jit(solution)/shard_map/ppermute | solution.py:12
  68.2 61.8 %collective-permute-start.2 = (bf16[256,3,2,128]{3,0,2,1:T(8,128)(2,1)}, bf16[256,3,2,128]{3,0,2,1:T(8,128)(2,1)}, u32[]{:S(2)}, u32[]{:S(2)}) collective-permute-start(bf16[256,3,2,128]{3,0,2,1:T(8,128)(2,1)} %get-tuple-element.18), channel_id=1, source_target_pairs={{0,8},{8,16},{16,24},{24,32},{32,40},{40,48},{48,56},{56,64},{64,7... | collective-permute-start | bytes 1179656 | tf_op jit(solution)/shard_map/ppermute | solution.py:12
  69.2 65.0 %collective-permute-start.3 = (bf16[256,3,2,128]{3,0,2,1:T(8,128)(2,1)}, bf16[256,3,2,128]{3,0,2,1:T(8,128)(2,1)}, u32[]{:S(2)}, u32[]{:S(2)}) collective-permute-start(bf16[256,3,2,128]{3,0,2,1:T(8,128)(2,1)} %get-tuple-element.17), channel_id=1, source_target_pairs={{0,248},{8,0},{16,8},{24,16},{32,24},{40,32},{48,40},{56,48},{64,5... | collective-permute-start | bytes 1179656 | tf_op jit(solution)/shard_map/ppermute | solution.py:12
  70.2 68.0 %collective-permute-start.4 = (bf16[256,3,2,128]{3,0,2,1:T(8,128)(2,1)}, bf16[256,3,2,128]{3,0,2,1:T(8,128)(2,1)}, u32[]{:S(2)}, u32[]{:S(2)}) collective-permute-start(bf16[256,3,2,128]{3,0,2,1:T(8,128)(2,1)} %get-tuple-element.16), channel_id=1, source_target_pairs={{0,240},{8,248},{16,0},{24,8},{32,16},{40,24},{48,32},{56,40},{64,... | collective-permute-start | bytes 1179656 | tf_op jit(solution)/shard_map/ppermute | solution.py:12
  80.1 0.8 copy-start.3
  80.9 63.3 %collective-permute-start.5 = (bf16[256,3,2,128]{3,0,2,1:T(8,128)(2,1)}, bf16[256,3,2,128]{3,0,2,1:T(8,128)(2,1)}, u32[]{:S(2)}, u32[]{:S(2)}) collective-permute-start(bf16[256,3,2,128]{3,0,2,1:T(8,128)(2,1)} %get-tuple-element.15), channel_id=1, source_target_pairs={{0,232},{8,240},{16,248},{24,0},{32,8},{40,16},{48,24},{56,32},{64... | collective-permute-start | bytes 1179656 | tf_op jit(solution)/shard_map/ppermute | solution.py:12
  148.3 4.3 %copy-start.1 = (bf16[1,256,3,256]{3,1,2,0:T(8,128)(2,1)S(1)}, bf16[1,256,3,256]{3,1,2,0:T(8,128)(2,1)}, u32[]{:S(2)}) copy-start(bf16[1,256,3,256]{3,1,2,0:T(8,128)(2,1)} %stack.55) | copy-start | bytes 1179652
  148.3 5.1 %copy-start.2 = (bf16[1,256,3,256]{3,1,2,0:T(8,128)(2,1)S(1)}, bf16[1,256,3,256]{3,1,2,0:T(8,128)(2,1)}, u32[]{:S(2)}) copy-start(bf16[1,256,3,256]{3,1,2,0:T(8,128)(2,1)} %stack.56) | copy-start | bytes 1179652
where the time goes:
time: 207 us; the launch traced here: 205 us
  local copies, waits for them, and re-layouts  87.1 us (42%)
  blocking collectives  43 us (21%)
  starting transfers between devices  38 us (18%)
  matrix products  19.7 us (10%)
  other arithmetic  11.3 us (5%)
  waiting for transfers between devices  5.94 us (3%)
    all_to_all x1, blocking collectives, on_device(): lax.all_to_all(packed_blocks, 'grp', split_axis=0, concat_axis=0, tiled=T...  43 us
    ppermute x6, starting transfers between devices, passed_along(): return lax.ppermute(value, axis, pairs)  38 us
    unnamed x30, local copies, waits for them, and re-layouts  25.9 us
    ppermute x6, local copies, waits for them, and re-layouts, passed_along(): return lax.ppermute(value, axis, pairs)  12.1 us
    another operation x7, local copies, waits for them, and re-layouts, on_device(): incoming = jnp.stack(pieces).reshape(slots, margin, set_count, 2 * width)  11 us
    gather x2, local copies, waits for them, and re-layouts, on_device(): imaged[slot_rows]  10.1 us
    dot_general x3, matrix products, complex_apply(): jnp.dot(matrix[1], flat, preferred_element_type=jnp.float32)  8.89 us
    gather x1, local copies, waits for them, and re-layouts, on_device(): projector = vectors[slot_rows].reshape(slots, margin, set_count, 2 * width)  8.4 us
  transfers between devices with their start and end apart: 6, of which 1 were waited for; matrix products, arithmetic and copies ran while one was open for 17% of the time, Pallas kernels for 0%

commit v1 on v0

v1 whole, which is shorter than its diff:
```python
import functools

import jax
import jax.numpy as jnp
from jax import lax
from jax.experimental import pallas as pl
from jax.experimental.pallas import tpu as pltpu
from jax.sharding import PartitionSpec as P

OFFSETS = (-3, -2, -1, 1, 2, 3)
MESH = pl.DeviceIdType.MESH
F32, BF16 = jnp.float32, jnp.bfloat16


def kernel(
    n_dom, n_grp, sets, width, tile,
    z_hbm, inv_hbm, op_hbm, rows_hbm, nb_ref, cnt_ref, own_ref,
    out_ref,
    zb, zw, inv, op, rows, upright, cols, hot, start, work, image, proj, qs, qr, blocks, rs,
    z_sem, inv_sem, op_sem, rows_sem, qs_sem, qr_sem, rs_sem, rr_sem, own_sem,
):
    slots, margin, edges = hot.shape
    steps = edges // tile
    parts = 2 * sets
    strip = 256
    half = width // 2
    dom, grp = lax.axis_index("dom"), lax.axis_index("grp")

    def matrix_load(source, target, sem, i, part):
        at = pl.multiple_of(i * tile, tile)
        return pltpu.make_async_copy(
            source.at[part, pl.ds(at, tile)],
            target.at[pl.ds(at, tile), pl.ds(part * edges, edges)],
            sem.at[i, part],
        )

    def z_load(i):
        at = pl.multiple_of(i * strip * parts, strip * parts)
        return pltpu.make_async_copy(
            z_hbm.at[pl.ds(at, strip * parts)], zb.at[pl.ds(at, strip * parts)], z_sem.at[i]
        )

    rows_load = pltpu.make_async_copy(rows_hbm, rows, rows_sem)
    rows_load.start()
    for i in range(edges // strip):
        z_load(i).start()

    def load(source, target, sem):
        for i in range(steps):
            for part in range(2):
                matrix_load(source, target, sem, i, part).start()

    load(inv_hbm, inv, inv_sem)

    barrier = pltpu.get_barrier_semaphore()
    for offset in OFFSETS:
        pl.semaphore_signal(
            barrier, inc=1, device_id=(lax.rem(dom + offset + n_dom, n_dom), grp), device_id_type=MESH
        )
    for j in range(1, n_grp):
        pl.semaphore_signal(
            barrier, inc=1, device_id=(dom, lax.rem(grp + j, n_grp)), device_id_type=MESH
        )

    def each(count, body):
        def run(i, carry):
            body(i)
            return carry

        lax.fori_loop(0, count, run, 0)

    def split(q, i, count=tile):
        at = pl.multiple_of(i * count, count)
        real = zw[pl.ds(at * parts + 2 * q, count, stride=parts), :].astype(BF16)
        imag = zw[pl.ds(at * parts + 2 * q + 1, count, stride=parts), :].astype(BF16)
        start[q, pl.ds(at, count), :] = jnp.concatenate([real, imag], axis=1)
        start[q, pl.ds(edges + at, count), :] = jnp.concatenate([-imag, real], axis=1)

    def unpack(i):
        z_load(i).wait()
        at = pl.multiple_of(i * strip * parts, strip * parts)
        zw[pl.ds(at, strip * parts), :] = zb[pl.ds(at, strip * parts), :].astype(F32)
        split(0, i, strip)

    each(edges // strip, unpack)
    load(op_hbm, op, op_sem)

    rows_load.wait()
    upright[...] = jnp.zeros_like(upright)
    for n in range(slots):
        upright[n : n + 1, :] = rows[n]
    cols[...] = jnp.transpose(upright[...])
    part_rows = margin // steps

    def make_hot(i):
        at = pl.multiple_of(i * part_rows, part_rows)
        position = at + lax.broadcasted_iota(jnp.int32, (part_rows, 1), 0)
        lane = lax.broadcasted_iota(jnp.int32, (part_rows, edges), 1)
        for n in range(slots):
            live = jnp.where(nb_ref[0, n] >= 0, cnt_ref[0, n], 0)
            picked = jnp.where(position < live, cols[pl.ds(at, part_rows), n : n + 1], -1)
            hot[n, pl.ds(at, part_rows), :] = jnp.where(lane == picked, 1.0, 0.0).astype(BF16)

    def product(matrix, source, i):
        at = pl.multiple_of(i * tile, tile)
        total = jnp.dot(matrix[pl.ds(at, tile), :], source[...], preferred_element_type=F32)
        rounded = total.astype(BF16)
        return at, rounded[:, :width], rounded[:, width:]

    def apply(matrix, source, target, i):
        at, real, imag = product(matrix, source, i)
        target[pl.ds(at, tile), :] = jnp.concatenate([real, imag], axis=1)
        target[pl.ds(edges + at, tile), :] = jnp.concatenate([-imag, real], axis=1)

    low = lax.broadcasted_iota(jnp.int32, (1, width), 1) < half

    def apply_last(source, i):
        at = pl.multiple_of(i * tile, tile)
        total = jnp.dot(op[pl.ds(at, tile), :], source[...], preferred_element_type=F32)
        real, imag = total[:, :width], total[:, width:]
        image[pl.ds(at, tile), :width] = jnp.where(low, real, pltpu.roll(imag, half, 1)).astype(BF16)
        image[pl.ds(at, tile), width:] = jnp.where(low, pltpu.roll(real, half, 1), imag).astype(BF16)

    pieces = [(q, h) for q in range(sets) for h in (0, 1)]
    ahead = 4

    def rows_out(p, n):
        q, h = pieces[p]
        return pltpu.make_async_remote_copy(
            src_ref=qs.at[q, n, h],
            dst_ref=qr.at[q, slots - 1 - n, h],
            send_sem=qs_sem.at[p, n],
            recv_sem=qr_sem.at[p, slots - 1 - n],
            device_id=(lax.rem(dom + OFFSETS[n] + n_dom, n_dom), grp),
            device_id_type=MESH,
        )

    def block_out(p, j):
        q, h = pieces[p]
        return pltpu.make_async_remote_copy(
            src_ref=rs.at[q, j, h],
            dst_ref=out_ref.at[grp, q, h],
            send_sem=rs_sem.at[p, j],
            recv_sem=rr_sem.at[p, j],
            device_id=(dom, lax.rem(grp + j, n_grp)),
            device_id_type=MESH,
        )

    for q in range(sets):

        def first(i):
            if q == 0:
                matrix_load(inv_hbm, inv, inv_sem, i, 0).wait()
                matrix_load(inv_hbm, inv, inv_sem, i, 1).wait()
                make_hot(i)
            apply(inv, start.at[q], work.at[0], i)

        def second(i):
            if q == 0:
                for other in range(1, sets):
                    split(other, i)
            apply(inv, work.at[0], work.at[1], i)

        def third(i):
            if q == 0:
                matrix_load(op_hbm, op, op_sem, i, 0).wait()
                matrix_load(op_hbm, op, op_sem, i, 1).wait()
            apply_last(work.at[1], i)

        each(steps, first)
        each(steps, second)
        each(steps, third)
        if q == 0:
            pl.semaphore_wait(barrier, slots + n_grp - 1)
        for n in range(slots):
            gathered = jnp.dot(hot[n], image[...], preferred_element_type=F32).astype(BF16)
            qs[q, n, 0] = gathered[:, :width]
            qs[q, n, 1] = gathered[:, width:]
            if 2 * q < ahead:
                rows_out(2 * q, n).start()
        if 2 * q + 1 < ahead:
            for n in range(slots):
                rows_out(2 * q + 1, n).start()

    def project(q, n):
        gathered = jnp.dot(hot[n], start[q, pl.ds(0, edges), :], preferred_element_type=F32)
        proj[q, n] = gathered.astype(BF16)

    for q in range(sets):
        each(slots, functools.partial(project, q))

    blocks[slots] = jnp.zeros(blocks.shape[1:], BF16)
    chosen = []
    for j in range(n_grp):
        there = lax.rem(grp + j, n_grp)
        pick = jnp.int32(slots)
        for n in reversed(range(slots)):
            pick = jnp.where(own_ref[0, n] == there, n, pick)
        chosen.append(pick)

    def couple(q, h, n):
        gram = lax.dot_general(
            proj[q, n], qr[q, n, h], (((0,), (0,)), ((), ())), preferred_element_type=F32
        )
        turned = pltpu.roll(gram[width:], half, 1)
        blocks[n] = (gram[:width] + jnp.where(low, -turned, turned)).astype(BF16)

    def block_kept(q):
        return pltpu.make_async_copy(rs.at[q, 0], out_ref.at[grp, q], own_sem.at[q])

    for p, (q, h) in enumerate(pieces):
        more = p + ahead < len(pieces)
        if more:
            for n in range(slots):
                rows_out(p, slots - 1 - n).wait_recv()
            for n in range(slots):
                rows_out(p + ahead, n).start()
        for n in range(slots):
            if not more:
                rows_out(p, slots - 1 - n).wait_recv()
            couple(q, h, n)
        for j in range(1, n_grp):
            rs[q, j, h] = blocks[chosen[j]]
            block_out(p, j).start()
        rs[q, 0, h] = blocks[chosen[0]]
        if h:
            block_kept(q).start()
    for q in range(sets):
        block_kept(q).wait()
    for p in range(len(pieces)):
        for j in range(1, n_grp):
            block_out(p, j).wait()
        for n in range(slots):
            rows_out(p, n).wait_send()


def widen(packed, out, wide, out_sem):
    count, sets, _, _, width = packed.shape
    half = width // 2
    low = lax.broadcasted_iota(jnp.int32, (1, width), 1) < half

    def store(i):
        return pltpu.make_async_copy(wide.at[i], out.at[i], out_sem.at[i])

    def one_source(i, carry):
        for q in range(sets):
            one, two = packed[i, q, 0].astype(F32), packed[i, q, 1].astype(F32)
            wide[i, q, 0] = jnp.where(low, one, pltpu.roll(two, half, 1))
            wide[i, q, 1] = jnp.where(low, pltpu.roll(one, half, 1), two)
        store(i).start()
        return carry

    lax.fori_loop(0, count, one_source, 0)
    for i in range(count):
        store(i).wait()


def solution(mesh):
    n_dom, n_grp = mesh.shape["dom"], mesh.shape["grp"]

    def on_device(deflation, inverse, operator, neighbours, counts, margin_rows, owners):
        _, edges, sets, _, width = deflation.shape
        slots, margin = margin_rows.shape[1:]
        tile = 512
        steps = edges // tile
        any_space = pl.BlockSpec(memory_space=pl.ANY)
        smem = pl.BlockSpec(memory_space=pltpu.SMEM)
        vmem = pltpu.VMEM
        dma = pltpu.SemaphoreType.DMA
        packed = pl.pallas_call(
            functools.partial(kernel, n_dom, n_grp, sets, width, tile),
            out_shape=pltpu.VMEM((n_grp, sets, 2, width, width), BF16),
            in_specs=[pl.BlockSpec(memory_space=pltpu.HBM)] * 4 + [smem] * 3,
            out_specs=pl.BlockSpec(memory_space=pltpu.VMEM),
            scratch_shapes=[
                vmem((edges * sets * 2, width), BF16),
                vmem((edges * sets * 2, width), F32),
                vmem((edges, 2 * edges), BF16),
                vmem((edges, 2 * edges), BF16),
                vmem((slots, 1, margin), jnp.int32),
                vmem((8, margin), jnp.int32),
                vmem((margin, 8), jnp.int32),
                vmem((slots, margin, edges), BF16),
                vmem((sets, 2 * edges, 2 * width), BF16),
                vmem((2, 2 * edges, 2 * width), BF16),
                vmem((edges, 2 * width), BF16),
                vmem((sets, slots, margin, 2 * width), BF16),
                vmem((sets, slots, 2, margin, width), BF16),
                vmem((sets, slots, 2, margin, width), BF16),
                vmem((slots + 1, width, width), BF16),
                vmem((sets, n_grp, 2, width, width), BF16),
                dma((edges // 256,)),
                dma((steps, 2)),
                dma((steps, 2)),
                dma,
                dma((2 * sets, slots)),
                dma((2 * sets, slots)),
                dma((2 * sets, n_grp)),
                dma((2 * sets, n_grp)),
                dma((sets,)),
            ],
            compiler_params=pltpu.CompilerParams(
                collective_id=0, has_side_effects=True, vmem_limit_bytes=61 * 2**20
            ),
        )(
            deflation.reshape(edges * sets * 2, width),
            inverse[0],
            operator[0],
            margin_rows.reshape(slots, 1, margin),
            neighbours,
            counts,
            owners[:, :, 0],
        )
        return pl.pallas_call(
            widen,
            out_shape=jax.ShapeDtypeStruct(packed.shape, F32),
            in_specs=[pl.BlockSpec(memory_space=pltpu.VMEM)],
            out_specs=any_space,
            scratch_shapes=[vmem(packed.shape, F32), dma((n_grp,))],
            compiler_params=pltpu.CompilerParams(vmem_limit_bytes=16 * 2**20),
        )(packed)

    whole = P(("dom", "grp"))
    return jax.shard_map(
        on_device, mesh=mesh, in_specs=(whole,) * 7, out_specs=whole, check_vma=False
    )
```

time: 207 us -> 59.6 us (0.29)
  the two profiles are of different devices: /device:TPU:16 before, /device:TPU:1 now
where the time goes in v1:
time: 59.6 us; the launch traced here: 59.5 us
  Pallas kernels  59.3 us (99%)
    pallas_call x1, Pallas kernels, on_device(): pl.pallas_call(functools.partial(kernel, n_dom, n_grp, sets, width, tile)...  57.5 us
    pallas_call x1, Pallas kernels, on_device(): pl.pallas_call(widen, out_shape=jax.ShapeDtypeStruct(packed.shape, F32),...  1.84 us

profile of v1, /device:TPU:1, one launch (start us, length us, event | category | flops | bytes accessed | tf_op | source)
XLA Modules:
  0.0 59.5 jit_solution(8048352998067911256)
XLA Ops:
  0.0 57.5 %shard_map.73.packed = bf16[8,3,2,128,128]{4,3,2,1,0:T(8,128)(2,1)S(1)} custom-call(bf16[6144,128]{1,0:T(8,128)(2,1)} %bitcast.7, bf16[2,1024,1024]{2,1,0:T(8,128)(2,1)} %bitcast.5, bf16[2,1024,1024]{2,1,0:T(8,128)(2,1)} %bitcast.6, s32[6,1,256]{2,1,0:T(1,128)} %bitcast.8, s32[1,6]{1,0:T(1,128)} %nb_ref.1, s32[1,6]{1,0:T(1,128)} %cnt_ref.1, s32[1,6]{1,0:T(1,128)} %bitcast.9), custom_call_target="tpu_custom_call" | custom-call | tf_op jit(solution)/shard_map/pallas_call | solution.py:270
  57.5 1.8 %shard_map.74 = f32[8,3,2,128,128]{4,3,2,1,0:T(8,128)} custom-call(bf16[8,3,2,128,128]{4,3,2,1,0:T(8,128)(2,1)S(1)} %shard_map.73.packed), custom_call_target="tpu_custom_call" | custom-call | tf_op jit(solution)/shard_map/pallas_call | solution.py:314

commit v2 on v1

--- a/solution.py
+++ b/solution.py
@@ -8,16 +8,18 @@
 from jax.sharding import PartitionSpec as P
 
 OFFSETS = (-3, -2, -1, 1, 2, 3)
+SERVED = (1, 4, 0, 5, 2, 3)
 MESH = pl.DeviceIdType.MESH
 F32, BF16 = jnp.float32, jnp.bfloat16
 
 
 def kernel(
     n_dom, n_grp, sets, width, tile,
-    z_hbm, inv_hbm, op_hbm, rows_hbm, nb_ref, cnt_ref, own_ref,
+    z_hbm, inv_hbm, op_hbm, rows_hbm, nb_hbm, cnt_hbm, own_hbm,
     out_ref,
     zb, zw, inv, op, rows, upright, cols, hot, start, work, image, proj, qs, qr, blocks, rs,
-    z_sem, inv_sem, op_sem, rows_sem, qs_sem, qr_sem, rs_sem, rr_sem, own_sem,
+    nb_ref, cnt_ref, own_ref,
+    z_sem, inv_sem, op_sem, rows_sem, small_sem, qs_sem, qr_sem, rs_sem, rr_sem, own_sem,
 ):
     slots, margin, edges = hot.shape
     steps = edges // tile
@@ -42,6 +44,12 @@
 
     rows_load = pltpu.make_async_copy(rows_hbm, rows, rows_sem)
     rows_load.start()
+    small = [
+        pltpu.make_async_copy(source, target, small_sem.at[i])
+        for i, (source, target) in enumerate(((nb_hbm, nb_ref), (cnt_hbm, cnt_ref), (own_hbm, own_ref)))
+    ]
+    for copy in small:
+        copy.start()
     for i in range(edges // strip):
         z_load(i).start()
 
@@ -86,6 +94,8 @@
     load(op_hbm, op, op_sem)
 
     rows_load.wait()
+    for copy in small:
+        copy.wait()
     upright[...] = jnp.zeros_like(upright)
     for n in range(slots):
         upright[n : n + 1, :] = rows[n]
@@ -99,7 +109,9 @@
         for n in range(slots):
             live = jnp.where(nb_ref[0, n] >= 0, cnt_ref[0, n], 0)
             picked = jnp.where(position < live, cols[pl.ds(at, part_rows), n : n + 1], -1)
-            hot[n, pl.ds(at, part_rows), :] = jnp.where(lane == picked, 1.0, 0.0).astype(BF16)
+            hot[n, pl.ds(at, part_rows), :] = jnp.where(
+                lane.astype(jnp.int16) == picked.astype(jnp.int16), jnp.ones((), BF16), jnp.zeros((), BF16)
+            )
 
     def product(matrix, source, i):
         at = pl.multiple_of(i * tile, tile)
@@ -122,7 +134,7 @@
         image[pl.ds(at, tile), width:] = jnp.where(low, pltpu.roll(real, half, 1), imag).astype(BF16)
 
     pieces = [(q, h) for q in range(sets) for h in (0, 1)]
-    ahead = 4
+    ahead = 3
 
     def rows_out(p, n):
         q, h = pieces[p]
@@ -186,9 +198,6 @@
         gathered = jnp.dot(hot[n], start[q, pl.ds(0, edges), :], preferred_element_type=F32)
         proj[q, n] = gathered.astype(BF16)
 
-    for q in range(sets):
-        each(slots, functools.partial(project, q))
-
     blocks[slots] = jnp.zeros(blocks.shape[1:], BF16)
     chosen = []
     for j in range(n_grp):
@@ -208,30 +217,38 @@
     def block_kept(q):
         return pltpu.make_async_copy(rs.at[q, 0], out_ref.at[grp, q], own_sem.at[q])
 
+    def settle(p):
+        q, h = pieces[p]
+        if h:
+            block_kept(q).wait()
+        for n in range(slots):
+            rows_out(p, n).wait_send()
+        for j in range(1, n_grp):
+            block_out(p, j).wait_send()
+
+    settled = 2
+    far_first = sorted(range(1, n_grp), key=lambda j: -min(j, n_grp - j))
     for p, (q, h) in enumerate(pieces):
-        more = p + ahead < len(pieces)
-        if more:
-            for n in range(slots):
-                rows_out(p, slots - 1 - n).wait_recv()
-            for n in range(slots):
+        if p >= settled:
+            settle(p - settled)
+        if h == 0:
+            each(slots, functools.partial(project, q))
+        for n in SERVED:
+            rows_out(p, slots - 1 - n).wait_recv()
+            if p + ahead < len(pieces):
                 rows_out(p + ahead, n).start()
-        for n in range(slots):
-            if not more:
-                rows_out(p, slots - 1 - n).wait_recv()
             couple(q, h, n)
-        for j in range(1, n_grp):
+        for j in far_first:
             rs[q, j, h] = blocks[chosen[j]]
             block_out(p, j).start()
         rs[q, 0, h] = blocks[chosen[0]]
         if h:
             block_kept(q).start()
-    for q in range(sets):
-        block_kept(q).wait()
+    for p in range(len(pieces) - settled, len(pieces)):
+        settle(p)
     for p in range(len(pieces)):
         for j in range(1, n_grp):
-            block_out(p, j).wait()
-        for n in range(slots):
-            rows_out(p, n).wait_send()
+            block_out(p, j).wait_recv()
 
 
 def widen(packed, out, wide, out_sem):
@@ -264,13 +281,12 @@
         tile = 512
         steps = edges // tile
         any_space = pl.BlockSpec(memory_space=pl.ANY)
-        smem = pl.BlockSpec(memory_space=pltpu.SMEM)
         vmem = pltpu.VMEM
         dma = pltpu.SemaphoreType.DMA
         packed = pl.pallas_call(
             functools.partial(kernel, n_dom, n_grp, sets, width, tile),
             out_shape=pltpu.VMEM((n_grp, sets, 2, width, width), BF16),
-            in_specs=[pl.BlockSpec(memory_space=pltpu.HBM)] * 4 + [smem] * 3,
+            in_specs=[pl.BlockSpec(memory_space=pltpu.HBM)] * 7,
             out_specs=pl.BlockSpec(memory_space=pltpu.VMEM),
             scratch_shapes=[
                 vmem((edges * sets * 2, width), BF16),
@@ -289,10 +305,14 @@
                 vmem((sets, slots, 2, margin, width), BF16),
                 vmem((slots + 1, width, width), BF16),
                 vmem((sets, n_grp, 2, width, width), BF16),
+                pltpu.SMEM((1, slots), jnp.int32),
+                pltpu.SMEM((1, slots), jnp.int32),
+                pltpu.SMEM((1, slots), jnp.int32),
                 dma((edges // 256,)),
                 dma((steps, 2)),
                 dma((steps, 2)),
                 dma,
+                dma((3,)),
                 dma((2 * sets, slots)),
                 dma((2 * sets, slots)),
                 dma((2 * sets, n_grp)),

time: 59.6 us -> 58.6 us (0.983)
  Pallas kernels: 59.3 us -> 58.4 us
    pallas_call x1, Pallas kernels: 57.5 us -> 56.5 us  [on_device(): pl.pallas_call(functools.partial(kernel, n_dom, n_grp, sets, width, tile)...]
where the time goes in v2:
time: 58.6 us; the launch traced here: 58.5 us
  Pallas kernels  58.4 us (100%)
    pallas_call x1, Pallas kernels, on_device(): pl.pallas_call(functools.partial(kernel, n_dom, n_grp, sets, width, tile)...  56.5 us
    pallas_call x1, Pallas kernels, on_device(): pl.pallas_call(widen, out_shape=jax.ShapeDtypeStruct(packed.shape, F32),...  1.84 us

profile of v2, /device:TPU:1, one launch (start us, length us, event | category | flops | bytes accessed | tf_op | source)
XLA Modules:
  0.0 58.5 jit_solution(2901034851068357033)
XLA Ops:
  0.0 56.5 %shard_map.73.packed = bf16[8,3,2,128,128]{4,3,2,1,0:T(8,128)(2,1)S(1)} custom-call(bf16[6144,128]{1,0:T(8,128)(2,1)} %bitcast.7, bf16[2,1024,1024]{2,1,0:T(8,128)(2,1)} %bitcast.5, bf16[2,1024,1024]{2,1,0:T(8,128)(2,1)} %bitcast.6, s32[6,1,256]{2,1,0:T(1,128)} %bitcast.8, s32[1,6]{1,0:T(1,128)} %nb_hbm.1, s32[1,6]{1,0:T(1,128)} %cnt_hbm.1, s32[1,6]{1,0:T(1,128)} %bitcast.9), custom_call_target="tpu_custom_call" | custom-call | tf_op jit(solution)/shard_map/pallas_call | solution.py:286
  56.5 1.8 %shard_map.74 = f32[8,3,2,128,128]{4,3,2,1,0:T(8,128)} custom-call(bf16[8,3,2,128,128]{4,3,2,1,0:T(8,128)(2,1)S(1)} %shard_map.73.packed), custom_call_target="tpu_custom_call" | custom-call | tf_op jit(solution)/shard_map/pallas_call | solution.py:334

commit v3 on v2

--- a/solution.py
+++ b/solution.py
@@ -184,14 +184,14 @@
         each(steps, third)
         if q == 0:
             pl.semaphore_wait(barrier, slots + n_grp - 1)
-        for n in range(slots):
+        for n in SERVED:
             gathered = jnp.dot(hot[n], image[...], preferred_element_type=F32).astype(BF16)
             qs[q, n, 0] = gathered[:, :width]
             qs[q, n, 1] = gathered[:, width:]
             if 2 * q < ahead:
                 rows_out(2 * q, n).start()
         if 2 * q + 1 < ahead:
-            for n in range(slots):
+            for n in SERVED:
                 rows_out(2 * q + 1, n).start()
 
     def project(q, n):

time: 58.6 us -> 61 us (1.041)
  the two profiles are of different devices: /device:TPU:1 before, /device:TPU:224 now
where the time goes in v3:
time: 61 us; the launch traced here: 60.9 us
  Pallas kernels  60.8 us (100%)
    pallas_call x1, Pallas kernels, on_device(): pl.pallas_call(functools.partial(kernel, n_dom, n_grp, sets, width, tile)...  58.9 us
    pallas_call x1, Pallas kernels, on_device(): pl.pallas_call(widen, out_shape=jax.ShapeDtypeStruct(packed.shape, F32),...  1.84 us

profile of v3, /device:TPU:224, one launch (start us, length us, event | category | flops | bytes accessed | tf_op | source)
XLA Modules:
  0.0 60.9 jit_solution(7705716758451596433)
XLA Ops:
  0.0 58.9 %shard_map.73.packed = bf16[8,3,2,128,128]{4,3,2,1,0:T(8,128)(2,1)S(1)} custom-call(bf16[6144,128]{1,0:T(8,128)(2,1)} %bitcast.7, bf16[2,1024,1024]{2,1,0:T(8,128)(2,1)} %bitcast.5, bf16[2,1024,1024]{2,1,0:T(8,128)(2,1)} %bitcast.6, s32[6,1,256]{2,1,0:T(1,128)} %bitcast.8, s32[1,6]{1,0:T(1,128)} %nb_hbm.1, s32[1,6]{1,0:T(1,128)} %cnt_hbm.1, s32[1,6]{1,0:T(1,128)} %bitcast.9), custom_call_target="tpu_custom_call" | custom-call | tf_op jit(solution)/shard_map/pallas_call | solution.py:286
  58.9 1.8 %shard_map.74 = f32[8,3,2,128,128]{4,3,2,1,0:T(8,128)} custom-call(bf16[8,3,2,128,128]{4,3,2,1,0:T(8,128)(2,1)S(1)} %shard_map.73.packed), custom_call_target="tpu_custom_call" | custom-call | tf_op jit(solution)/shard_map/pallas_call | solution.py:334
